TPU v7x, 32 devices: a whole 2x2x4 slice. The times are simulated.
32 devices in a mesh: groups: 2 (over y), ctx: 4 (over z), inner: 2 (over x), chan: 2 (over core).
Axes of the slice: x: 2, y: 2, z: 4, core: 2. Of those that a mesh axis runs over, the one named last changes fastest.
Arguments:
- queries: bfloat16 [2048, 8192], P(('groups', 'ctx', 'inner'), 'chan'), parts along dimension 0, may hold values from -6 to 6
- keys_in: bfloat16 [2048, 8192], P(('groups', 'ctx', 'inner'), 'chan'), parts along dimension 0, may hold values from -6 to 6
- values_in: bfloat16 [2048, 8192], P(('groups', 'ctx', 'inner'), 'chan'), parts along dimension 0, may hold values from -6 to 6
- out_grad: bfloat16 [2048, 8192], P(('groups', 'ctx', 'inner'), 'chan'), parts along dimension 0, may hold values from -6 to 6
- short_taps: float32 [3, 7, 8192], P(None, None, 'chan'), may hold values from -2 to 2
- pole_rate: float32 [16, 512], P(None, 'chan'), may hold values from 0.0001953125 to 0.15, as said below
- residue: float32 [16, 512], P(None, 'chan'), may hold values from -0.55 to 0.55
Outputs:
- query_grad: bfloat16 [2048, 8192], P(('groups', 'ctx', 'inner'), 'chan'), parts along dimension 0
- key_grad: bfloat16 [2048, 8192], P(('groups', 'ctx', 'inner'), 'chan'), parts along dimension 0
- value_grad: bfloat16 [2048, 8192], P(('groups', 'ctx', 'inner'), 'chan'), parts along dimension 0
- tap_grad: float32 [6, 7, 8192], P('groups', None, 'chan'), parts along dimension 0
- rate_grad: float32 [32, 512], P('groups', 'chan'), parts along dimension 0
- residue_grad: float32 [32, 512], P('groups', 'chan'), parts along dimension 0
There are 2 independent parts, one for each index of `groups`. A program takes and returns all parts, laid end to end along the dimension named above; an argument that names none is the same for every part. Nothing has to cross between parts.
Inputs may be any that keep to these rules, and one draw needn't show every extreme that they name: `pole_rate`: each rate lies between 0.2 / 1024 and 0.15.
All inputs are finite; a program needn't handle non-finite values.
Results may differ from a plain program's by a relative error of at most 0.001.
Values may be sent and summed in bfloat16 or wider, within the bound.
A program may use at most 192 MiB of HBM per device.

v0:
```python
import jax
import jax.numpy as jnp
from jax import lax
from jax.sharding import PartitionSpec as P


def shifted(block, axis, distance):
    devices = range(lax.axis_size(axis))
    route = [(i - distance, i) for i in devices if i - distance in devices]
    return lax.ppermute(block, axis, route)


def carried_in_2(part, axis, combine, identity, reverse):
    count = lax.axis_size(axis)
    place = lax.axis_index(axis)
    ahead = count - 1 - place if reverse else place
    gathered = jax.tree.map(lambda a: lax.all_gather(a, axis), part)
    state = jax.tree.map(lambda a, e: jnp.zeros_like(a) + jnp.asarray(e, a.dtype), part, identity)

    def one(lap, state):
        source = count - 1 - lap if reverse else lap
        return combine(
            state, jax.tree.map(lambda a: lax.dynamic_index_in_dim(a, source, 0, False), gathered)
        )

    return lax.fori_loop(0, ahead, one, state)


def affine_join(earlier, later):
    ratio = later[0]
    carried = earlier[1]
    shape = carried.shape
    scaled = (carried.reshape(shape[0], ratio.shape[1], -1) * ratio[:, :, None]).reshape(shape)
    return (earlier[0] * ratio, scaled + later[1])


def spread(table, members):
    return jnp.repeat(table, members, axis=1)


def causal_mix(extended, taps, row_count):
    tap_count = taps.shape[0]
    running = taps[tap_count - 1] * extended[0:row_count]
    for lag_index in range(tap_count - 2, -1, -1):
        offset_row = tap_count - 1 - lag_index
        running = running + taps[lag_index] * extended[offset_row : offset_row + row_count]
    return running


def ahead_mix(extended, taps, row_count):
    tap_count = taps.shape[0]
    running = taps[0] * extended[0:row_count]
    for lag_index in range(1, tap_count):
        running = running + taps[lag_index] * extended[lag_index : lag_index + row_count]
    return running


def tap_terms(grad_mix, extended, tap_count, row_count):
    collected = []
    for lag_index in range(tap_count):
        offset_row = tap_count - 1 - lag_index
        collected.append(jnp.sum(grad_mix * extended[offset_row : offset_row + row_count], axis=0))
    return jnp.stack(collected, axis=0)


def on_device(queries, keys_in, values_in, out_grad, short_taps, pole_rate, residue):
    row_count, chan_count = queries.shape
    mode_count, local_groups = pole_rate.shape
    members = chan_count // local_groups
    tap_count = short_taps.shape[1]
    tail_rows = tap_count - 1
    devices = lax.axis_size(("ctx", "inner"))
    token_total = row_count * devices
    before = shifted(
        (
            queries[row_count - tail_rows :],
            keys_in[row_count - tail_rows :],
            values_in[row_count - tail_rows :],
        ),
        ("ctx", "inner"),
        1,
    )
    query_wide = jnp.concatenate([before[0], queries], axis=0).astype(jnp.float32)
    key_wide = jnp.concatenate([before[1], keys_in], axis=0).astype(jnp.float32)
    value_wide = jnp.concatenate([before[2], values_in], axis=0).astype(jnp.float32)
    query_mix = causal_mix(query_wide, short_taps[0], row_count)
    key_mix = causal_mix(key_wide, short_taps[1], row_count)
    value_mix = causal_mix(value_wide, short_taps[2], row_count)
    source_term = key_mix * value_mix
    grad_out = out_grad.astype(jnp.float32)
    adjoint_term = grad_out * query_mix
    lam_table = jnp.exp(-pole_rate)
    lam_rows = spread(lam_table, members)
    residue_rows = spread(residue, members)
    block_rows = 16
    block_count = row_count // block_rows
    src_blocks = source_term.reshape(block_count, block_rows, chan_count)
    adj_blocks = adjoint_term.reshape(block_count, block_rows, chan_count)
    zero_state = jnp.zeros((mode_count, chan_count), jnp.float32)

    def local_forward(state_carry, src_blk):
        following = state_carry
        for step_row in range(block_rows):
            following = lam_rows * following + src_blk[step_row]
        return (following, state_carry)

    local_final, local_starts = lax.scan(local_forward, zero_state, src_blocks)

    def local_backward(adj_carry, adj_blk):
        for step_row in range(block_rows - 1, -1, -1):
            adj_carry = lam_rows * adj_carry + adj_blk[step_row]
        return (adj_carry, None)

    local_first = lax.scan(local_backward, zero_state, adj_blocks, reverse=True)[0]
    rate_dev = pole_rate * float(row_count)
    decay_dev = jnp.exp(-rate_dev)
    neutral = (jnp.ones_like(decay_dev), jnp.zeros_like(local_final))
    state_in = carried_in_2(
        (decay_dev, local_final), ("ctx", "inner"), affine_join, neutral, False
    )[1]
    adjoint_in = carried_in_2(
        (decay_dev, local_first), ("ctx", "inner"), affine_join, neutral, True
    )[1]
    offsets = jnp.arange(block_count, dtype=jnp.float32) * float(block_rows)
    start_scale = spread(
        jnp.exp(-pole_rate[None, :, :] * offsets[:, None, None]).reshape(
            block_count * mode_count, local_groups
        ),
        members,
    ).reshape(block_count, mode_count, chan_count)
    block_starts = local_starts + start_scale * state_in[None]

    def retreat(carried_in, inputs):
        later_adj, mode_sum, rate_sum = carried_in
        src_blk, adj_blk, block_start = inputs
        states = []
        running = block_start
        out_rows = []
        for step_row in range(block_rows):
            running = lam_rows * running + src_blk[step_row]
            states.append(running)
            out_rows.append(jnp.sum(residue_rows * running, axis=0))
        adjoint = later_adj
        adj_rows = [None] * block_rows
        for step_row in range(block_rows - 1, -1, -1):
            adj_row = adj_blk[step_row]
            adjoint = lam_rows * adjoint + adj_row
            adj_rows[step_row] = jnp.sum(residue_rows * adjoint, axis=0)
            mode_sum = mode_sum + adj_row * states[step_row]
            earlier = block_start if step_row == 0 else states[step_row - 1]
            rate_sum = rate_sum + adjoint * earlier
        return (
            (adjoint, mode_sum, rate_sum),
            (jnp.stack(out_rows, axis=0), jnp.stack(adj_rows, axis=0)),
        )

    initial = (adjoint_in, zero_state, zero_state)
    carried, produced = lax.scan(
        retreat, initial, (src_blocks, adj_blocks, block_starts), reverse=True
    )
    long_out = produced[0].reshape(row_count, chan_count)
    long_adj = produced[1].reshape(row_count, chan_count)
    mode_grad = jnp.sum(carried[1].reshape(mode_count, local_groups, members), axis=2)
    rate_total = jnp.sum(carried[2].reshape(mode_count, local_groups, members), axis=2)
    pole_grad = -lam_table * residue * rate_total
    query_back = grad_out * long_out
    key_back = long_adj * value_mix
    value_back = long_adj * key_mix
    next_heads = shifted(
        (query_back[:tail_rows], key_back[:tail_rows], value_back[:tail_rows]), ("ctx", "inner"), -1
    )
    query_grad = ahead_mix(
        jnp.concatenate([query_back, next_heads[0]], axis=0), short_taps[0], row_count
    ).astype(jnp.bfloat16)
    key_grad = ahead_mix(
        jnp.concatenate([key_back, next_heads[1]], axis=0), short_taps[1], row_count
    ).astype(jnp.bfloat16)
    value_grad = ahead_mix(
        jnp.concatenate([value_back, next_heads[2]], axis=0), short_taps[2], row_count
    ).astype(jnp.bfloat16)
    tap_local = jnp.stack(
        [
            tap_terms(query_back, query_wide, tap_count, row_count),
            tap_terms(key_back, key_wide, tap_count, row_count),
            tap_terms(value_back, value_wide, tap_count, row_count),
        ],
        axis=0,
    )
    reduced = lax.psum((tap_local, mode_grad, pole_grad), ("ctx", "inner"))
    tap_grad = reduced[0] / jnp.sqrt(jnp.float32(token_total))
    residue_grad = reduced[1] / jnp.float32(token_total)
    rate_grad = reduced[2] / jnp.float32(token_total)
    return (query_grad, key_grad, value_grad, tap_grad, rate_grad, residue_grad)


def solution(mesh):
    placed = (
        P(("groups", "ctx", "inner"), "chan"),
        P(("groups", "ctx", "inner"), "chan"),
        P(("groups", "ctx", "inner"), "chan"),
        P(("groups", "ctx", "inner"), "chan"),
        P(None, None, "chan"),
        P(None, "chan"),
        P(None, "chan"),
    )
    return jax.shard_map(
        on_device,
        mesh=mesh,
        in_specs=placed,
        out_specs=(
            P(("groups", "ctx", "inner"), "chan"),
            P(("groups", "ctx", "inner"), "chan"),
            P(("groups", "ctx", "inner"), "chan"),
            P("groups", None, "chan"),
            P("groups", "chan"),
            P("groups", "chan"),
        ),
        check_vma=False,
    )
```

profile of v0, /device:TPU:0, one launch (start us, length us, event | category | flops | bytes accessed | tf_op | source)
XLA Modules:
  0.0 732.9 jit_solution(7204519826283749657)
XLA Ops:
  8.1 4.8 collective-permute-start.1
  14.4 3.4 collective-permute-start.2
  19.4 4.0 collective-permute-start
  28.6 8.5 %broadcast_in_dim.40 = f32[128,256,16]{2,1,0:T(8,128)} broadcast(f32[128,256]{1,0:T(8,128)S(1)} %fusion.109), dimensions={0,1} | broadcast | bytes 2228224 | tf_op jit(solution)/shard_map/broadcast_in_dim | solution.py:38
  37.1 15.2 %reshape_reshape.3 = f32[8,16,4096]{2,1,0:T(8,128)} reshape(f32[128,256,16]{2,1,0:T(8,128)} %broadcast_in_dim.40) | data formatting | bytes 4194304 | tf_op jit(solution)/shard_map/reshape;reshape | solution.py:130
  52.3 30.5 %all-gather = f32[128,256]{1,0:T(8,128)S(1)} all-gather(f32[16,256]{1,0:T(8,128)S(1)} %get-tuple-element.784), channel_id=2, replica_groups=mesh['groups'=2,'ctx'=4,'inner'=2,'chan'=2] {'ctx','inner'}, dimensions={0}, use_global_device_ids=true | all-gather | bytes 147456 | tf_op jit(solution)/shard_map/all_gather | solution.py:17
  86.0 4.9 fusion.110
  92.5 73.8 %while.80 = (s32[]{:T(128)}, f32[16,4096]{1,0:T(8,128)S(1)}, f32[8,16,4096]{2,1,0:T(8,128)}, f32[8,16,4096]{2,1,0:T(8,128)}, f32[16,256]{1,0:T(8,128)}, /*index=...) while((s32[]{:T(128)}, f32[16,4096]{1,0:T(8,128)S(1)}, ...), condition=%wide.region_5.6_spmd.clone, body=%wide.region_4.5_spmd.clone.sunk | while | flops 2228242 | bytes 2900932 | solution.py:107
  172.1 68.2 %while.79 = (s32[]{:T(128)}, f32[16,4096]{1,0:T(8,128)S(1)}, f32[8,16,4096]{2,1,0:T(8,128)}, f32[16,256]{1,0:T(8,128)}, s32[]{:T(128)}, /*index=5*/s32[]{:T(128)...) while((s32[]{:T(128)}, f32[16,4096]{1,0:T(8,128)S(1)}, ...), condition=%wide.region_1.2_spmd.clone, body=%wide.region_0.1_spmd.clone.sunk | while | flops 2162707 | bytes 2376143 | solution.py:114
  241.2 47.2 %all-gather.6.cloned.1.call-done = f32[128,4096]{1,0:T(8,128)} async-done(((f32[16,4096]{1,0:T(8,128)}), f32[128,4096]{1,0:T(8,128)}) %all-gather.6.cloned.1.call-update) | async-done | bytes 2097168 | tf_op jit(solution)/shard_map/all_gather | solution.py:17
  288.4 43.5 %while.77 = (s32[]{:T(128)}, f32[16,4096]{1,0:T(8,128)S(1)}, s32[]{:T(128)}, f32[8,16,256]{2,1,0:T(8,128)S(1)}, f32[8,16,4096]{2,1,0:T(8,128)}, /*index=5*/s32[]{:T(128)}, s32[]{:T(128)}, s32[]{:T(128)}, s32[]{:T(128)}) while((s32[]{:T(128)}, f32[16,4096]{1,0:T(8,128)S(1)}, s32[]{:T(128)}, f32[8,16,256]{2,1,0:T(8,128)S(1)}, ...), condition=%wide.region_3.4_spmd, body=%wide.region_2.3_spmd.sunk | while | flops 131078 | bytes 1884307 | solution.py:26
  331.9 3.8 multiply_add_fusion.33
  338.8 290.6 %while.81 = (s32[]{:T(128)}, f32[16,4096]{1,0:T(8,128)S(1)}, f32[16,4096]{1,0:T(8,128)}, f32[16,4096]{1,0:T(8,128)}, f32[8,16,4096]{2,1,0:T(8,128)}, /*index=5*/...) while((s32[]{:T(128)}, f32[16,4096]{1,0:T(8,128)S(1)}, ...), condition=%wide.region_41.42_spmd.clone, body=%wide.region_8.41_spmd.clone.sunk | while | flops 18874388 | bytes 16942528 | solution.py:158
  400.7 3.3 stack.454
  436.8 3.3 stack.454
  508.9 3.3 stack.454
  545.5 3.3 stack.454
  582.3 3.3 stack.454
  618.9 3.3 stack.454
  638.2 10.3 %multiply_reduce_fusion.46 = (f32[4096]{0:T(1024)S(1)}, f32[4096]{0:T(1024)S(1)}, f32[4096]{0:T(1024)S(1)}, f32[4096]{0:T(1024)S(1)}, f32[4096]{0:T(1024)S(1)}, ...) fusion(f32[134,4096]{1,0:T(8,128)} %copy-done.2, f32[8,16,4096]{2,1,0:T(8,128)} %get-tuple-element.471, ...), kind=kLoop, calls=%fused_computation.291 | loop fusion | flops 8359936 | bytes 20037632 | tf_op jit(solution)/shard_map/reduce_sum | solution.py:62
  648.6 5.7 multiply_reduce_fusion.32
  663.7 37.2 %all-reduce = (f32[16,256]{1,0:T(8,128)S(1)}, f32[16,256]{1,0:T(8,128)S(1)}) all-reduce(f32[16,256]{1,0:T(8,128)S(1)} %copy-done.86, f32[16,256]{1,0:T(8,128)S(1)} %reduce_sum.709), channel_id=1, replica_groups=mesh['groups'=2,'ctx'=4,'inner'=2,'chan'=2] {'ctx','inner'}, use_global_device_ids=true, to_apply=%region_65.66 | all-reduce | flops 8192 | bytes 65536 | tf_op jit(solution)/shard_map/psum | solution.py:189
  701.6 8.7 %fusion.59 = bf16[128,4096]{1,0:T(8,128)(2,1)} fusion(f32[6,4096]{1,0:T(8,128)S(1)} %collective-permute-done.5, f32[128,4096]{1,0:T(8,128)} %get-tuple-element.683, f32[4096]{0:T(1024)S(1)} %bitcast.601, f32[4096]{0:T(1024)S(1)} %bitcast.599, f32[4096]{0:T(1024)S(1)} %bitcast.589, f32[4096]{0:T(1024)S(1)} %bitcast.591, f32[4096]{0:T(1024)S(1)} %bitcast.593, ...), kind=kLoop, calls=%fused_computation.213 | loop fusion | flops 10485760 | bytes 3358720 | tf_op jit(solution)/shard_map/convert_element_type | solution.py:180
  716.6 7.8 %all-reduce.3.cloned.1.call-done = f32[3,7,4096]{2,1,0:T(8,128)} async-done(((f32[3,7,4096]{2,1,0:T(8,128)}), f32[3,7,4096]{2,1,0:T(8,128)}) %all-reduce.3.cloned.1.call-update) | async-done | bytes 344080 | tf_op jit(solution)/shard_map/psum | solution.py:189
  (878 shorter events, 501.1 us)
Async XLA Ops:
  7.2 234.0 %all-gather.8.cloned.1.call-start = ((), (), s32[]{:S(2)}) async-start(), calls=%async_computation.2 | async-start | bytes 2359296 | tf_op jit(solution)/shard_map/all_gather | solution.py:17
  8.1 74.7 %collective-permute-start.1 = (bf16[6,4096]{1,0:T(8,128)(2,1)S(1)}, bf16[6,4096]{1,0:T(8,128)(2,1)S(1)}, u32[]{:S(2)}, u32[]{:S(2)}) collective-permute-start(bf16[6,4096]{1,0:T(8,128)(2,1)S(1)} %slice.848), channel_id=1, source_target_pairs={{0,2},{2,4},{4,6},{6,8},{8,10},{10,12},{12,14},{1,3},{3,5},{5,7},{... | collective-permute-start | bytes 147464 | tf_op jit(solution)/shard_map/ppermute | solution.py:10
  14.4 69.9 %collective-permute-start.2 = (bf16[6,4096]{1,0:T(8,128)(2,1)}, bf16[6,4096]{1,0:T(8,128)(2,1)S(1)}, u32[]{:S(2)}, u32[]{:S(2)}) collective-permute-start(bf16[6,4096]{1,0:T(8,128)(2,1)} %slice.863), channel_id=1, source_target_pairs={{0,2},{2,4},{4,6},{6,8},{8,10},{10,12},{12,14},{1,3},{3,5},{5,7},{... | collective-permute-start | bytes 147464 | tf_op jit(solution)/shard_map/ppermute | solution.py:10
  19.4 148.2 %collective-permute-start = (bf16[6,4096]{1,0:T(8,128)(2,1)}, bf16[6,4096]{1,0:T(8,128)(2,1)}, u32[]{:S(2)}, u32[]{:S(2)}) collective-permute-start(bf16[6,4096]{1,0:T(8,128)(2,1)} %slice.834), channel_id=1, source_target_pairs={{0,2},{2,4},{4,6},{6,8},{8,10},{10,12},{12,14},{1,3},{3,5},{5,7},{... | collective-permute-start | bytes 147464 | tf_op jit(solution)/shard_map/ppermute | solution.py:10
  25.7 60.2 %copy-start.44 = (f32[1,1,4096]{2,1,0:T(1,128)}, f32[1,1,4096]{2,1,0:T(1,128)S(1)}, u32[]{:S(2)}) copy-start(f32[1,1,4096]{2,1,0:T(1,128)S(1)} %get-tuple-element.761) | copy-start | bytes 49156
  25.7 60.2 %copy-start.46 = (f32[1,1,4096]{2,1,0:T(1,128)}, f32[1,1,4096]{2,1,0:T(1,128)S(1)}, u32[]{:S(2)}) copy-start(f32[1,1,4096]{2,1,0:T(1,128)S(1)} %get-tuple-element.767) | copy-start | bytes 49156
  25.7 60.2 %copy-start.48 = (f32[1,1,4096]{2,1,0:T(1,128)}, f32[1,1,4096]{2,1,0:T(1,128)S(1)}, u32[]{:S(2)}) copy-start(f32[1,1,4096]{2,1,0:T(1,128)S(1)} %get-tuple-element.768) | copy-start | bytes 49156
  25.7 60.2 %copy-start.50 = (f32[1,1,4096]{2,1,0:T(1,128)}, f32[1,1,4096]{2,1,0:T(1,128)S(1)}, u32[]{:S(2)}) copy-start(f32[1,1,4096]{2,1,0:T(1,128)S(1)} %get-tuple-element.769) | copy-start | bytes 49156
  25.7 60.2 %copy-start.52 = (f32[1,1,4096]{2,1,0:T(1,128)}, f32[1,1,4096]{2,1,0:T(1,128)S(1)}, u32[]{:S(2)}) copy-start(f32[1,1,4096]{2,1,0:T(1,128)S(1)} %get-tuple-element.770) | copy-start | bytes 49156
  25.8 60.2 %copy-start.54 = (f32[1,1,4096]{2,1,0:T(1,128)}, f32[1,1,4096]{2,1,0:T(1,128)S(1)}, u32[]{:S(2)}) copy-start(f32[1,1,4096]{2,1,0:T(1,128)S(1)} %get-tuple-element.771) | copy-start | bytes 49156
  25.8 60.2 %copy-start.56 = (f32[1,1,4096]{2,1,0:T(1,128)}, f32[1,1,4096]{2,1,0:T(1,128)S(1)}, u32[]{:S(2)}) copy-start(f32[1,1,4096]{2,1,0:T(1,128)S(1)} %get-tuple-element.772) | copy-start | bytes 49156
  25.8 60.2 %copy-start.58 = (f32[1,1,4096]{2,1,0:T(1,128)}, f32[1,1,4096]{2,1,0:T(1,128)S(1)}, u32[]{:S(2)}) copy-start(f32[1,1,4096]{2,1,0:T(1,128)S(1)} %get-tuple-element.762) | copy-start | bytes 49156
  25.8 143.4 %copy-start.72 = (f32[1,1,4096]{2,1,0:T(1,128)}, f32[1,1,4096]{2,1,0:T(1,128)S(1)}, u32[]{:S(2)}) copy-start(f32[1,1,4096]{2,1,0:T(1,128)S(1)} %get-tuple-element.773) | copy-start | bytes 49156
  25.8 143.4 %copy-start.74 = (f32[1,1,4096]{2,1,0:T(1,128)}, f32[1,1,4096]{2,1,0:T(1,128)S(1)}, u32[]{:S(2)}) copy-start(f32[1,1,4096]{2,1,0:T(1,128)S(1)} %get-tuple-element.774) | copy-start | bytes 49156
  25.8 143.4 %copy-start.76 = (f32[1,1,4096]{2,1,0:T(1,128)}, f32[1,1,4096]{2,1,0:T(1,128)S(1)}, u32[]{:S(2)}) copy-start(f32[1,1,4096]{2,1,0:T(1,128)S(1)} %get-tuple-element.775) | copy-start | bytes 49156
  25.9 143.4 %copy-start.78 = (f32[1,1,4096]{2,1,0:T(1,128)}, f32[1,1,4096]{2,1,0:T(1,128)S(1)}, u32[]{:S(2)}) copy-start(f32[1,1,4096]{2,1,0:T(1,128)S(1)} %get-tuple-element.776) | copy-start | bytes 49156
  25.9 143.4 %copy-start.80 = (f32[1,1,4096]{2,1,0:T(1,128)}, f32[1,1,4096]{2,1,0:T(1,128)S(1)}, u32[]{:S(2)}) copy-start(f32[1,1,4096]{2,1,0:T(1,128)S(1)} %get-tuple-element.777) | copy-start | bytes 49156
  25.9 143.4 %copy-start.82 = (f32[1,1,4096]{2,1,0:T(1,128)}, f32[1,1,4096]{2,1,0:T(1,128)S(1)}, u32[]{:S(2)}) copy-start(f32[1,1,4096]{2,1,0:T(1,128)S(1)} %get-tuple-element.778) | copy-start | bytes 49156
  25.9 143.4 %copy-start.84 = (f32[1,1,4096]{2,1,0:T(1,128)}, f32[1,1,4096]{2,1,0:T(1,128)S(1)}, u32[]{:S(2)}) copy-start(f32[1,1,4096]{2,1,0:T(1,128)S(1)} %get-tuple-element.779) | copy-start | bytes 49156
  167.0 121.4 %all-gather.6.cloned.1.call-start = ((), (), s32[]{:S(2)}) async-start(), calls=%async_computation.1 | async-start | bytes 2359296 | tf_op jit(solution)/shard_map/all_gather | solution.py:17
  241.1 483.3 %all-reduce.3.cloned.1.call-start = ((), (), s32[]{:S(2)}) async-start(), calls=%async_computation | async-start | bytes 786432 | tf_op jit(solution)/shard_map/psum | solution.py:189
  656.6 44.9 %collective-permute-start.5 = (f32[6,4096]{1,0:T(8,128)S(1)}, f32[6,4096]{1,0:T(8,128)S(1)}, u32[]{:S(2)}, u32[]{:S(2)}) collective-permute-start(f32[6,4096]{1,0:T(8,128)S(1)} %slice.1005), channel_id=1, source_target_pairs={{2,0},{4,2},{6,4},{8,6},{10,8},{12,10},{14,12},{3,1},{5,3},{7,5},{... | collective-permute-start | bytes 294920 | tf_op jit(solution)/shard_map/ppermute | solution.py:10
  657.9 52.4 %collective-permute-start.4 = (f32[6,4096]{1,0:T(8,128)S(1)}, f32[6,4096]{1,0:T(8,128)S(1)}, u32[]{:S(2)}, u32[]{:S(2)}) collective-permute-start(f32[6,4096]{1,0:T(8,128)S(1)} %slice.994), channel_id=1, source_target_pairs={{2,0},{4,2},{6,4},{8,6},{10,8},{12,10},{14,12},{3,1},{5,3},{7,5},{... | collective-permute-start | bytes 294920 | tf_op jit(solution)/shard_map/ppermute | solution.py:10
  660.2 53.3 %collective-permute-start.3 = (f32[6,4096]{1,0:T(8,128)S(1)}, f32[6,4096]{1,0:T(8,128)S(1)}, u32[]{:S(2)}, u32[]{:S(2)}) collective-permute-start(f32[6,4096]{1,0:T(8,128)S(1)} %slice.983), channel_id=1, source_target_pairs={{2,0},{4,2},{6,4},{8,6},{10,8},{12,10},{14,12},{3,1},{5,3},{7,5},{... | collective-permute-start | bytes 294920 | tf_op jit(solution)/shard_map/ppermute | solution.py:10
  (289 other events, 2835.0 us)
Sparse Core Ops, SparseCore 0:
  167.2 47.1 all-gather.7
  241.2 47.2 all-gather.5
  655.8 68.4 all-reduce.2
where the time goes:
time: 747 us; the launch traced here: 733 us
  local copies, waits for them, and re-layouts  411 us (55%)
  other arithmetic  163 us (22%)
  blocking collectives  67.7 us (9%)
  waiting for transfers between devices  55.1 us (7%)
  starting transfers between devices  16.8 us (2%)
  between operations  15 us (2%)
    reshape x32, local copies, waits for them, and re-layouts, spread(): return jnp.repeat(table, members, axis=1)  101 us
    broadcast_in_dim x33, local copies, waits for them, and re-layouts, spread(): return jnp.repeat(table, members, axis=1)  92.8 us
    all_gather x2, waiting for transfers between devices, carried_in_2(): gathered = jax.tree.map(lambda a: lax.all_gather(a, axis), part)  47.3 us
    psum x1, blocking collectives, on_device(): reduced = lax.psum((tap_local, mode_grad, pole_grad), ('ctx', 'inner'))  37.2 us
    mul x21, local copies, waits for them, and re-layouts, affine_join(): carried.reshape(shape[0], ratio.shape[1], -1) * ratio[:, :, None]  35.7 us
    all_gather x1, blocking collectives, carried_in_2(): gathered = jax.tree.map(lambda a: lax.all_gather(a, axis), part)  30.5 us
    reduce_sum x16, other arithmetic, retreat(): out_rows.append(jnp.sum(residue_rows * running, axis=0))  29.3 us
    another operation x8, local copies, waits for them, and re-layouts, retreat(): jnp.stack(adj_rows, axis=0)  26.7 us
  transfers between devices with their start and end apart: 9, of which 2 were waited for; matrix products, arithmetic and copies ran while one was open for 28% of the time, Pallas kernels for 0%

commit v1 on v0

--- a/solution.py
+++ b/solution.py
@@ -186,7 +186,7 @@
         ],
         axis=0,
     )
-    reduced = lax.psum((tap_local, mode_grad, pole_grad), ("ctx", "inner"))
+    reduced = lax.psum(lax.psum((tap_local, mode_grad, pole_grad), "ctx"), "inner")
     tap_grad = reduced[0] / jnp.sqrt(jnp.float32(token_total))
     residue_grad = reduced[1] / jnp.float32(token_total)
     rate_grad = reduced[2] / jnp.float32(token_total)

time: 747 us -> 753 us (level)
    psum x1 -> x2, blocking collectives: 37.2 us -> 30.3 us  [the longest x1 21.2 us: on_device(): lax.psum((tap_local, mode_grad, pole_grad), 'ctx')]
  transfers between devices with their start and end apart: 9 -> 10, of which waited for: 2 -> 2; matrix products, arithmetic and copies ran while one was open for 28% -> 29% of each run, Pallas kernels for 0% -> 0%
where the time goes in v1:
time: 753 us; the launch traced here: 738 us
  local copies, waits for them, and re-layouts  411 us (55%)
  other arithmetic  169 us (22%)
  waiting for transfers between devices  61.7 us (8%)
  blocking collectives  60.8 us (8%)
  starting transfers between devices  16.8 us (2%)
  between operations  15 us (2%)
    reshape x32, local copies, waits for them, and re-layouts, spread(): return jnp.repeat(table, members, axis=1)  101 us
    broadcast_in_dim x33, local copies, waits for them, and re-layouts, spread(): return jnp.repeat(table, members, axis=1)  92.8 us
    all_gather x2, waiting for transfers between devices, carried_in_2(): gathered = jax.tree.map(lambda a: lax.all_gather(a, axis), part)  47.3 us
    mul x21, local copies, waits for them, and re-layouts, affine_join(): carried.reshape(shape[0], ratio.shape[1], -1) * ratio[:, :, None]  35.7 us
    all_gather x1, blocking collectives, carried_in_2(): gathered = jax.tree.map(lambda a: lax.all_gather(a, axis), part)  30.5 us
    reduce_sum x16, other arithmetic, retreat(): out_rows.append(jnp.sum(residue_rows * running, axis=0))  29.3 us
    another operation x8, local copies, waits for them, and re-layouts, retreat(): jnp.stack(adj_rows, axis=0)  26.7 us
    another operation x8, local copies, waits for them, and re-layouts, retreat(): jnp.stack(out_rows, axis=0)  25.9 us
  transfers between devices with their start and end apart: 10, of which 2 were waited for; matrix products, arithmetic and copies ran while one was open for 29% of the time, Pallas kernels for 0%

profile of v1, /device:TPU:0, one launch (start us, length us, event | category | flops | bytes accessed | tf_op | source)
XLA Modules:
  0.0 738.4 jit_solution(17317236535521957448)
XLA Ops:
  8.1 4.8 collective-permute-start.1
  14.4 3.4 collective-permute-start.2
  19.4 4.0 collective-permute-start
  28.6 8.5 %broadcast_in_dim.40 = f32[128,256,16]{2,1,0:T(8,128)} broadcast(f32[128,256]{1,0:T(8,128)S(1)} %fusion.109), dimensions={0,1} | broadcast | bytes 2228224 | tf_op jit(solution)/shard_map/broadcast_in_dim | solution.py:38
  37.1 15.2 %reshape_reshape.3 = f32[8,16,4096]{2,1,0:T(8,128)} reshape(f32[128,256,16]{2,1,0:T(8,128)} %broadcast_in_dim.40) | data formatting | bytes 4194304 | tf_op jit(solution)/shard_map/reshape;reshape | solution.py:130
  52.3 30.5 %all-gather = f32[128,256]{1,0:T(8,128)S(1)} all-gather(f32[16,256]{1,0:T(8,128)S(1)} %get-tuple-element.786), channel_id=2, replica_groups=mesh['groups'=2,'ctx'=4,'inner'=2,'chan'=2] {'ctx','inner'}, dimensions={0}, use_global_device_ids=true | all-gather | bytes 147456 | tf_op jit(solution)/shard_map/all_gather | solution.py:17
  86.0 4.9 fusion.110
  92.5 73.8 %while.80 = (s32[]{:T(128)}, f32[16,4096]{1,0:T(8,128)S(1)}, f32[8,16,4096]{2,1,0:T(8,128)}, f32[8,16,4096]{2,1,0:T(8,128)}, f32[16,256]{1,0:T(8,128)}, /*index=...) while((s32[]{:T(128)}, f32[16,4096]{1,0:T(8,128)S(1)}, ...), condition=%wide.region_5.6_spmd.clone, body=%wide.region_4.5_spmd.clone.sunk | while | flops 2228242 | bytes 2900932 | solution.py:107
  172.1 68.2 %while.79 = (s32[]{:T(128)}, f32[16,4096]{1,0:T(8,128)S(1)}, f32[8,16,4096]{2,1,0:T(8,128)}, f32[16,256]{1,0:T(8,128)}, s32[]{:T(128)}, /*index=5*/s32[]{:T(128)...) while((s32[]{:T(128)}, f32[16,4096]{1,0:T(8,128)S(1)}, ...), condition=%wide.region_1.2_spmd.clone, body=%wide.region_0.1_spmd.clone.sunk | while | flops 2162707 | bytes 2376143 | solution.py:114
  241.2 47.2 %all-gather.6.cloned.1.call-done = f32[128,4096]{1,0:T(8,128)} async-done(((f32[16,4096]{1,0:T(8,128)}), f32[128,4096]{1,0:T(8,128)}) %all-gather.6.cloned.1.call-update) | async-done | bytes 2097168 | tf_op jit(solution)/shard_map/all_gather | solution.py:17
  288.4 43.5 %while.77 = (s32[]{:T(128)}, f32[16,4096]{1,0:T(8,128)S(1)}, s32[]{:T(128)}, f32[8,16,256]{2,1,0:T(8,128)S(1)}, f32[8,16,4096]{2,1,0:T(8,128)}, /*index=5*/s32[]{:T(128)}, s32[]{:T(128)}, s32[]{:T(128)}, s32[]{:T(128)}) while((s32[]{:T(128)}, f32[16,4096]{1,0:T(8,128)S(1)}, s32[]{:T(128)}, f32[8,16,256]{2,1,0:T(8,128)S(1)}, ...), condition=%wide.region_3.4_spmd, body=%wide.region_2.3_spmd.sunk | while | flops 131078 | bytes 1884307 | solution.py:26
  331.9 3.8 multiply_add_fusion.33
  338.8 290.6 %while.81 = (s32[]{:T(128)}, f32[16,4096]{1,0:T(8,128)S(1)}, f32[16,4096]{1,0:T(8,128)}, f32[16,4096]{1,0:T(8,128)}, f32[8,16,4096]{2,1,0:T(8,128)}, /*index=5*/...) while((s32[]{:T(128)}, f32[16,4096]{1,0:T(8,128)S(1)}, ...), condition=%wide.region_41.42_spmd.clone, body=%wide.region_8.41_spmd.clone.sunk | while | flops 18874388 | bytes 16942528 | solution.py:158
  400.7 3.3 stack.454
  436.8 3.3 stack.454
  508.9 3.3 stack.454
  545.5 3.3 stack.454
  638.2 10.3 %multiply_reduce_fusion.46 = (f32[4096]{0:T(1024)S(1)}, f32[4096]{0:T(1024)S(1)}, f32[4096]{0:T(1024)S(1)}, f32[4096]{0:T(1024)S(1)}, f32[4096]{0:T(1024)S(1)}, ...) fusion(f32[134,4096]{1,0:T(8,128)} %copy-done.2, f32[8,16,4096]{2,1,0:T(8,128)} %get-tuple-element.471, ...), kind=kLoop, calls=%fused_computation.291 | loop fusion | flops 8359936 | bytes 20037632 | tf_op jit(solution)/shard_map/reduce_sum | solution.py:62
  648.6 5.7 multiply_reduce_fusion.32
  663.8 21.2 %all-reduce = (f32[16,256]{1,0:T(8,128)S(1)}, f32[16,256]{1,0:T(8,128)S(1)}) all-reduce(f32[16,256]{1,0:T(8,128)S(1)} %copy-done.85, f32[16,256]{1,0:T(8,128)S(1)} %reduce_sum.709), channel_id=1, replica_groups=mesh['groups'=2,'ctx'=4,'inner'=2,'chan'=2] {'ctx'}, use_global_device_ids=true, to_apply=%region_66.67 | all-reduce | flops 8192 | bytes 65536 | tf_op jit(solution)/shard_map/psum | solution.py:189
  685.0 9.0 %all-reduce.1 = (f32[16,256]{1,0:T(8,128)S(1)}, f32[16,256]{1,0:T(8,128)S(1)}) all-reduce(f32[16,256]{1,0:T(8,128)S(1)} %get-tuple-element.676, f32[16,256]{1,0:T(8,128)S(1)} %get-tuple-element.677), channel_id=1, replica_groups=mesh['groups'=2,'ctx'=4,'inner'=2,'chan'=2] {'inner'}, use_global_device_ids=true, to_apply=%region_67.68 | all-reduce | flops 8192 | bytes 65536 | tf_op jit(solution)/shard_map/psum | solution.py:189
  694.7 8.7 %fusion.59 = bf16[128,4096]{1,0:T(8,128)(2,1)} fusion(f32[6,4096]{1,0:T(8,128)S(1)} %collective-permute-done.5, f32[128,4096]{1,0:T(8,128)} %get-tuple-element.685, f32[4096]{0:T(1024)S(1)} %bitcast.601, f32[4096]{0:T(1024)S(1)} %bitcast.599, f32[4096]{0:T(1024)S(1)} %bitcast.589, f32[4096]{0:T(1024)S(1)} %bitcast.591, f32[4096]{0:T(1024)S(1)} %bitcast.593, ...), kind=kLoop, calls=%fused_computation.213 | loop fusion | flops 10485760 | bytes 3358720 | tf_op jit(solution)/shard_map/convert_element_type | solution.py:180
  706.7 8.8 %fusion.93 = bf16[128,4096]{1,0:T(8,128)(2,1)} fusion(f32[6,4096]{1,0:T(8,128)S(1)} %collective-permute-done.3, f32[128,4096]{1,0:T(8,128)} %get-tuple-element.683, f32[4096]{0:T(1024)S(1)} %bitcast.603, f32[4096]{0:T(1024)S(1)} %bitcast.605, f32[4096]{0:T(1024)S(1)} %bitcast.607, f32[4096]{0:T(1024)S(1)} %bitcast.609, f32[4096]{0:T(1024)S(1)} %bitcast.611, ...), kind=kLoop, calls=%fused_computation.247 | loop fusion | flops 10485760 | bytes 3358720 | tf_op jit(solution)/shard_map/convert_element_type | solution.py:174
  715.5 14.3 %all-reduce.7.cloned.1.call-done = f32[3,7,4096]{2,1,0:T(8,128)} async-done(((f32[3,7,4096]{2,1,0:T(8,128)}), f32[3,7,4096]{2,1,0:T(8,128)}) %all-reduce.7.cloned.1.call-update) | async-done | bytes 344080 | tf_op jit(solution)/shard_map/psum | solution.py:189
  (880 shorter events, 504.8 us)
Async XLA Ops:
  7.2 234.0 %all-gather.8.cloned.1.call-start = ((), (), s32[]{:S(2)}) async-start(), calls=%async_computation.3 | async-start | bytes 2359296 | tf_op jit(solution)/shard_map/all_gather | solution.py:17
  8.1 74.7 %collective-permute-start.1 = (bf16[6,4096]{1,0:T(8,128)(2,1)S(1)}, bf16[6,4096]{1,0:T(8,128)(2,1)S(1)}, u32[]{:S(2)}, u32[]{:S(2)}) collective-permute-start(bf16[6,4096]{1,0:T(8,128)(2,1)S(1)} %slice.848), channel_id=1, source_target_pairs={{0,2},{2,4},{4,6},{6,8},{8,10},{10,12},{12,14},{1,3},{3,5},{5,7},{... | collective-permute-start | bytes 147464 | tf_op jit(solution)/shard_map/ppermute | solution.py:10
  14.4 69.9 %collective-permute-start.2 = (bf16[6,4096]{1,0:T(8,128)(2,1)}, bf16[6,4096]{1,0:T(8,128)(2,1)S(1)}, u32[]{:S(2)}, u32[]{:S(2)}) collective-permute-start(bf16[6,4096]{1,0:T(8,128)(2,1)} %slice.863), channel_id=1, source_target_pairs={{0,2},{2,4},{4,6},{6,8},{8,10},{10,12},{12,14},{1,3},{3,5},{5,7},{... | collective-permute-start | bytes 147464 | tf_op jit(solution)/shard_map/ppermute | solution.py:10
  19.4 148.2 %collective-permute-start = (bf16[6,4096]{1,0:T(8,128)(2,1)}, bf16[6,4096]{1,0:T(8,128)(2,1)}, u32[]{:S(2)}, u32[]{:S(2)}) collective-permute-start(bf16[6,4096]{1,0:T(8,128)(2,1)} %slice.834), channel_id=1, source_target_pairs={{0,2},{2,4},{4,6},{6,8},{8,10},{10,12},{12,14},{1,3},{3,5},{5,7},{... | collective-permute-start | bytes 147464 | tf_op jit(solution)/shard_map/ppermute | solution.py:10
  25.7 60.2 %copy-start.43 = (f32[1,1,4096]{2,1,0:T(1,128)}, f32[1,1,4096]{2,1,0:T(1,128)S(1)}, u32[]{:S(2)}) copy-start(f32[1,1,4096]{2,1,0:T(1,128)S(1)} %get-tuple-element.763) | copy-start | bytes 49156
  25.7 60.2 %copy-start.45 = (f32[1,1,4096]{2,1,0:T(1,128)}, f32[1,1,4096]{2,1,0:T(1,128)S(1)}, u32[]{:S(2)}) copy-start(f32[1,1,4096]{2,1,0:T(1,128)S(1)} %get-tuple-element.769) | copy-start | bytes 49156
  25.7 60.2 %copy-start.47 = (f32[1,1,4096]{2,1,0:T(1,128)}, f32[1,1,4096]{2,1,0:T(1,128)S(1)}, u32[]{:S(2)}) copy-start(f32[1,1,4096]{2,1,0:T(1,128)S(1)} %get-tuple-element.770) | copy-start | bytes 49156
  25.7 60.2 %copy-start.49 = (f32[1,1,4096]{2,1,0:T(1,128)}, f32[1,1,4096]{2,1,0:T(1,128)S(1)}, u32[]{:S(2)}) copy-start(f32[1,1,4096]{2,1,0:T(1,128)S(1)} %get-tuple-element.771) | copy-start | bytes 49156
  25.7 60.2 %copy-start.51 = (f32[1,1,4096]{2,1,0:T(1,128)}, f32[1,1,4096]{2,1,0:T(1,128)S(1)}, u32[]{:S(2)}) copy-start(f32[1,1,4096]{2,1,0:T(1,128)S(1)} %get-tuple-element.772) | copy-start | bytes 49156
  25.8 60.2 %copy-start.53 = (f32[1,1,4096]{2,1,0:T(1,128)}, f32[1,1,4096]{2,1,0:T(1,128)S(1)}, u32[]{:S(2)}) copy-start(f32[1,1,4096]{2,1,0:T(1,128)S(1)} %get-tuple-element.773) | copy-start | bytes 49156
  25.8 60.2 %copy-start.55 = (f32[1,1,4096]{2,1,0:T(1,128)}, f32[1,1,4096]{2,1,0:T(1,128)S(1)}, u32[]{:S(2)}) copy-start(f32[1,1,4096]{2,1,0:T(1,128)S(1)} %get-tuple-element.774) | copy-start | bytes 49156
  25.8 143.4 %copy-start.71 = (f32[1,1,4096]{2,1,0:T(1,128)}, f32[1,1,4096]{2,1,0:T(1,128)S(1)}, u32[]{:S(2)}) copy-start(f32[1,1,4096]{2,1,0:T(1,128)S(1)} %get-tuple-element.775) | copy-start | bytes 49156
  25.8 143.4 %copy-start.73 = (f32[1,1,4096]{2,1,0:T(1,128)}, f32[1,1,4096]{2,1,0:T(1,128)S(1)}, u32[]{:S(2)}) copy-start(f32[1,1,4096]{2,1,0:T(1,128)S(1)} %get-tuple-element.776) | copy-start | bytes 49156
  25.8 143.4 %copy-start.75 = (f32[1,1,4096]{2,1,0:T(1,128)}, f32[1,1,4096]{2,1,0:T(1,128)S(1)}, u32[]{:S(2)}) copy-start(f32[1,1,4096]{2,1,0:T(1,128)S(1)} %get-tuple-element.777) | copy-start | bytes 49156
  25.9 143.4 %copy-start.77 = (f32[1,1,4096]{2,1,0:T(1,128)}, f32[1,1,4096]{2,1,0:T(1,128)S(1)}, u32[]{:S(2)}) copy-start(f32[1,1,4096]{2,1,0:T(1,128)S(1)} %get-tuple-element.778) | copy-start | bytes 49156
  25.9 143.4 %copy-start.79 = (f32[1,1,4096]{2,1,0:T(1,128)}, f32[1,1,4096]{2,1,0:T(1,128)S(1)}, u32[]{:S(2)}) copy-start(f32[1,1,4096]{2,1,0:T(1,128)S(1)} %get-tuple-element.779) | copy-start | bytes 49156
  25.9 143.4 %copy-start.81 = (f32[1,1,4096]{2,1,0:T(1,128)}, f32[1,1,4096]{2,1,0:T(1,128)S(1)}, u32[]{:S(2)}) copy-start(f32[1,1,4096]{2,1,0:T(1,128)S(1)} %get-tuple-element.780) | copy-start | bytes 49156
  25.9 143.4 %copy-start.83 = (f32[1,1,4096]{2,1,0:T(1,128)}, f32[1,1,4096]{2,1,0:T(1,128)S(1)}, u32[]{:S(2)}) copy-start(f32[1,1,4096]{2,1,0:T(1,128)S(1)} %get-tuple-element.781) | copy-start | bytes 49156
  167.0 121.4 %all-gather.6.cloned.1.call-start = ((), (), s32[]{:S(2)}) async-start(), calls=%async_computation.2 | async-start | bytes 2359296 | tf_op jit(solution)/shard_map/all_gather | solution.py:17
  241.1 465.6 %all-reduce.5.cloned.1.call-start = ((), (), s32[]{:S(2)}) async-start(), calls=%async_computation | async-start | bytes 786432 | tf_op jit(solution)/shard_map/psum | solution.py:189
  655.7 74.1 %all-reduce.7.cloned.1.call-start = ((), (), s32[]{:S(2)}) async-start(), calls=%async_computation.1 | async-start | bytes 786432 | tf_op jit(solution)/shard_map/psum | solution.py:189
  656.7 38.0 %collective-permute-start.5 = (f32[6,4096]{1,0:T(8,128)S(1)}, f32[6,4096]{1,0:T(8,128)S(1)}, u32[]{:S(2)}, u32[]{:S(2)}) collective-permute-start(f32[6,4096]{1,0:T(8,128)S(1)} %slice.1005), channel_id=1, source_target_pairs={{2,0},{4,2},{6,4},{8,6},{10,8},{12,10},{14,12},{3,1},{5,3},{7,5},{... | collective-permute-start | bytes 294920 | tf_op jit(solution)/shard_map/ppermute | solution.py:10
  658.0 45.5 %collective-permute-start.4 = (f32[6,4096]{1,0:T(8,128)S(1)}, f32[6,4096]{1,0:T(8,128)S(1)}, u32[]{:S(2)}, u32[]{:S(2)}) collective-permute-start(f32[6,4096]{1,0:T(8,128)S(1)} %slice.994), channel_id=1, source_target_pairs={{2,0},{4,2},{6,4},{8,6},{10,8},{12,10},{14,12},{3,1},{5,3},{7,5},{... | collective-permute-start | bytes 294920 | tf_op jit(solution)/shard_map/ppermute | solution.py:10
  660.2 46.5 %collective-permute-start.3 = (f32[6,4096]{1,0:T(8,128)S(1)}, f32[6,4096]{1,0:T(8,128)S(1)}, u32[]{:S(2)}, u32[]{:S(2)}) collective-permute-start(f32[6,4096]{1,0:T(8,128)S(1)} %slice.983), channel_id=1, source_target_pairs={{2,0},{4,2},{6,4},{8,6},{10,8},{12,10},{14,12},{3,1},{5,3},{7,5},{... | collective-permute-start | bytes 294920 | tf_op jit(solution)/shard_map/ppermute | solution.py:10
  (289 other events, 2796.2 us)
Sparse Core Ops, SparseCore 0:
  167.2 47.1 all-gather.7
  241.2 47.2 all-gather.5
  655.8 34.2 all-reduce.4
  706.8 23.0 all-reduce.6
